TPU v7x, 256 devices: a whole 4x4x8 slice. The times are simulated.
256 devices in a mesh: space: 16 (over z, core), tm: 16 (over y, x).
Axes of the slice: x: 4, y: 4, z: 8, core: 2. Of those that a mesh axis runs over, the one named last changes fastest.
Arguments:
- snapshots: bfloat16 [131072, 4096], P('space', 'tm'), may hold values from -6 to 6
- pod_basis: bfloat16 [131072, 512], P('space'), may hold values from -0.015625 to 0.015625
Outputs:
- hankel_gram: float32 [4096, 4096], P('tm', 'space')
All inputs are finite; a program needn't handle non-finite values.
Results may differ from a plain program's by a relative error of at most 0.0014.
Values may be sent and summed in bfloat16 or wider, within the bound.
A program may use at most 64 MiB of HBM per device.

v0:
```python
import jax
import jax.numpy as jnp
from jax import lax
from jax.sharding import PartitionSpec as P

MODES = 512
DELAYS = 64


def diagonal_sum(kernel, height, breadth):
    total = jnp.zeros((height, breadth), jnp.float32)
    for offset in range(DELAYS):
        total = total + kernel[offset : offset + height, offset : offset + breadth]
    return total


def per_device(snapshots, pod_basis):
    local_steps = snapshots.shape[1]
    all_steps = local_steps * lax.axis_size("tm")
    col_width = all_steps // lax.axis_size("space")
    partial_value = jnp.dot(pod_basis.T, snapshots, preferred_element_type=jnp.float32)
    row_start = lax.axis_index("tm") * local_steps
    coeffs = lax.psum(partial_value, "space").astype(jnp.bfloat16)
    col_start = lax.axis_index("space") * col_width
    all_coeffs = lax.all_gather(coeffs, "tm", axis=1, tiled=True)
    padded = jnp.concatenate(
        [all_coeffs, jnp.zeros((all_coeffs.shape[0], DELAYS), jnp.bfloat16)], axis=1
    )
    row_block = lax.dynamic_slice_in_dim(padded, row_start, local_steps + DELAYS, 1)
    col_block = lax.dynamic_slice_in_dim(padded, col_start, col_width + DELAYS, 1)
    kernel = jnp.dot(row_block.T, col_block, preferred_element_type=jnp.float32)
    hankel_gram = diagonal_sum(kernel, local_steps, col_width)
    return hankel_gram * (MODES * DELAYS) ** (-0.5)


def solution(mesh):
    in_specs = (P("space", "tm"), P("space", None))
    out_specs = P("tm", "space")
    return jax.shard_map(
        per_device, mesh=mesh, in_specs=in_specs, out_specs=out_specs, check_vma=False
    )
```

profile of v0, /device:TPU:1, one launch (start us, length us, event | category | flops | bytes accessed | tf_op | source)
XLA Modules:
  0.0 144.8 jit_solution(9650783201208145620)
XLA Ops:
  6.5 0.0 all-gather.2.cloned.1.call-start
  6.5 6.9 %fusion.4 = f32[512,256]{1,0:T(8,128)S(1)} fusion(bf16[8192,512]{1,0:T(8,128)(2,1)} %param.3, bf16[8192,256]{1,0:T(8,128)(2,1)} %param.2), kind=kOutput, calls=%fused_computation.69 | convolution fusion | flops 2147483648 | bytes 13107200 | tf_op jit(solution)/shard_map/dot_general | solution.py:21
  13.5 54.6 %all-reduce.2 = bf16[512,256]{1,0:T(8,128)(2,1)} all-reduce(f32[512,256]{1,0:T(8,128)S(1)} %fusion.4), channel_id=1, replica_groups=mesh['space'=16,'tm'=16] {'space'}, use_global_device_ids=true, to_apply=%region_0.0 | all-reduce | flops 131072 | bytes 786432 | tf_op jit(solution)/shard_map/psum | solution.py:23
  68.1 0.0 all-gather.2.cloned.1.call-update
  68.1 62.6 %all-gather.2.cloned.1.call-done = bf16[512,4096]{1,0:T(8,128)(2,1)} async-done(((bf16[512,256]{1,0:T(8,128)(2,1)}), bf16[512,4096]{1,0:T(8,128)(2,1)}) %all-gather.2.cloned.1.call-update) | async-done | bytes 4194320 | tf_op jit(solution)/shard_map/all_gather | solution.py:25
  130.7 1.9 %fusion = f32[320,320]{1,0:T(8,128)S(1)} fusion(s32[]{:T(128)S(6)} %select_n.6, bf16[512,4096]{1,0:T(8,128)(2,1)} %all-gather.2.cloned.1.call-done, s32[]{:T(128)S(6)} %select_n.7), kind=kOutput, calls=%fused_computation.2 | convolution fusion | flops 104857600 | bytes 8798216 | tf_op jit(solution)/shard_map/dot_general | solution.py:31
  132.5 5.4 %fusion.1 = f32[256,256]{1,0:T(8,128)} fusion(f32[320,320]{1,0:T(8,128)S(1)} %fusion), kind=kLoop, calls=%fused_computation.4 | loop fusion | flops 4194304 | bytes 17039360 | tf_op jit(solution)/shard_map/mul | solution.py:33
Async XLA Ops:
  6.5 124.1 %all-gather.2.cloned.1.call-start = ((), (), s32[]{:S(2)}) async-start(), calls=%async_computation | async-start | bytes 4456448 | tf_op jit(solution)/shard_map/all_gather | solution.py:25
Sparse Core Ops, SparseCore 0:
  68.2 62.4 all-gather.1
where the time goes:
time: 145 us
  waiting for transfers between devices  62.6 us (43%)
  blocking collectives  54.6 us (38%)
  between operations  13.4 us (9%)
  matrix products  8.78 us (6%)
  other arithmetic  5.43 us (4%)
    all_gather x1, waiting for transfers between devices, per_device(): all_coeffs = lax.all_gather(coeffs, 'tm', axis=1, tiled=True)  62.6 us
    psum x1, blocking collectives, per_device(): coeffs = lax.psum(partial_value, 'space').astype(jnp.bfloat16)  54.6 us
    dot_general x1, matrix products, per_device(): jnp.dot(pod_basis.T, snapshots, preferred_element_type=jnp.float32)  6.93 us
    mul x1, other arithmetic, per_device(): return hankel_gram * (MODES * DELAYS) ** (-0.5)  5.43 us
  transfers between devices with their start and end apart: 1, of which 1 were waited for; matrix products, arithmetic and copies ran while one was open for 0% of the time, Pallas kernels for 0%

commit v1 on v0

v1 whole, which is shorter than its diff:
```python
import jax
import jax.numpy as jnp
from jax import lax
from jax.experimental import pallas as pl
from jax.experimental.pallas import tpu as pltpu
from jax.sharding import PartitionSpec as P

MODES = 512
DELAYS = 64
MESH = pl.DeviceIdType.MESH
NZ = 8
NT = 16
STEPS = 256
POINTS = 8192
HALF = 256
PIECES = MODES // HALF
CHUNK = 16
OWN = STEPS // 2
KCUT = 4
KC = POINTS // KCUT
ROWS = STEPS + DELAYS
COLS = 384
SCALE = (MODES * DELAYS) ** -0.5


def kernel(
    snap,
    pod,
    out,
    sv,
    pv,
    acc,
    sib_buf,
    mine,
    rs_buf,
    ci,
    cj,
    s_sem,
    p_sem,
    sib_ss,
    sib_rs,
    rs_ss,
    rs_rs,
    za_ss,
    za_rs,
    sw_ss,
    sw_rs,
    rh_ss,
    rh_rs,
    fw_ss,
    fw_rs,
    sc_ss,
    sc_rs,
    hs_ss,
    hs_rs,
    ag_ss,
    ag_rs,
    ah_ss,
    ah_rs,
):
    space = lax.axis_index("space")
    tm = lax.axis_index("tm")
    z = space // 2
    core = lax.rem(space, 2)
    chunk_at = core * NZ + z

    sibling = {"space": z * 2 + 1 - core, "tm": tm}

    def z_peer(d):
        return {"space": lax.rem(z + d, NZ) * 2 + core, "tm": tm}

    def plane_peer(d):
        return {"space": space, "tm": lax.rem(tm + d, NT)}

    def owner_space(k):
        return lax.rem(k, NZ) * 2 + k // NZ

    scatter_to = {"space": tm, "tm": chunk_at}
    scatter_from = {"space": owner_space(tm), "tm": space}
    scatter_self = jnp.logical_and(chunk_at == tm, space == tm)
    odd_plane = lax.rem(space, 2)
    halo_owner = jnp.logical_and(chunk_at < 4, tm >= 1)
    halo_plane = lax.rem(tm + NT - 1, NT)
    halo_to = {
        "space": halo_plane,
        "tm": jnp.where(lax.rem(halo_plane, 2) == 0, 5 * chunk_at, 3 * chunk_at + 3)
        * jnp.where(halo_owner, 1, 0),
    }
    holds_even = jnp.logical_and(odd_plane == 0, lax.rem(tm, 5) == 0)
    holds_odd = jnp.logical_and(
        odd_plane == 1,
        jnp.logical_and(lax.rem(tm, 3) == 0, jnp.logical_and(tm >= 3, tm <= 12)),
    )
    has_next = space < NT - 1
    holder = jnp.logical_and(has_next, jnp.logical_or(holds_even, holds_odd))
    held_halo = jnp.where(
        holder, jnp.where(odd_plane == 0, tm // 5, tm // 3 - 1), 0
    )
    halo_from = {"space": held_halo * 2, "tm": lax.rem(space + 1, NT)}

    for k in range(KCUT):
        at = pl.ds(k * KC, KC)
        pltpu.make_async_copy(snap.at[at], sv.at[at], s_sem.at[k]).start()
        pltpu.make_async_copy(
            pod.at[at, pl.ds(0, HALF)], pv.at[0, at], p_sem.at[0, k]
        ).start()
    for p in range(1, PIECES):
        for k in range(KCUT):
            at = pl.ds(k * KC, KC)
            pltpu.make_async_copy(
                pod.at[at, pl.ds(p * HALF, HALF)], pv.at[p, at], p_sem.at[p, k]
            ).start()

    barrier = pltpu.get_barrier_semaphore()

    def greet(who):
        pl.semaphore_signal(barrier, inc=1, device_id=who, device_id_type=MESH)

    greet(sibling)
    for d in range(1, NZ):
        greet(z_peer(d))
    for d in range(1, NT):
        greet(plane_peer(d))

    @pl.when(jnp.logical_not(scatter_self))
    def _():
        greet(scatter_from)

    @pl.when(holder)
    def _():
        greet(halo_from)

    expected = (
        1
        + (NZ - 1)
        + (NT - 1)
        + jnp.where(scatter_self, 0, 1)
        + jnp.where(halo_owner, 1, 0)
    )

    cj[:, ROWS:, :] = jnp.zeros((PIECES, COLS - ROWS, HALF), jnp.bfloat16)

    @pl.when(space == NT - 1)
    def _():
        cj[:, STEPS:ROWS, :] = jnp.zeros((PIECES, DELAYS, HALF), jnp.bfloat16)

    @pl.when(tm == NT - 1)
    def _():
        ci[:, STEPS:ROWS, :] = jnp.zeros((PIECES, DELAYS, HALF), jnp.bfloat16)

    def multiply(p, k):
        at = pl.ds(k * KC, KC)
        if p == 0:
            pltpu.make_async_copy(snap.at[at], sv.at[at], s_sem.at[k]).wait()
        pltpu.make_async_copy(
            pod.at[at, pl.ds(p * HALF, HALF)], pv.at[p, at], p_sem.at[p, k]
        ).wait()
        term = lax.dot_general(
            sv[at],
            pv[p, at],
            (((0,), (0,)), ((), ())),
            preferred_element_type=jnp.float32,
        )
        if k == 0:
            acc[p] = term
        else:
            acc[p] += term

    def remote(src, dst, ss, rs, who):
        return pltpu.make_async_remote_copy(
            src_ref=src,
            dst_ref=dst,
            send_sem=ss,
            recv_sem=rs,
            device_id=who,
            device_id_type=MESH,
        )

    own_rows = pl.ds(pl.multiple_of(core * OWN, OWN), OWN)
    other_rows = pl.ds(pl.multiple_of((1 - core) * OWN, OWN), OWN)
    chunk_rows = pl.ds(pl.multiple_of(chunk_at * CHUNK, CHUNK), CHUNK)
    held_rows = pl.ds(pl.multiple_of(tm * CHUNK, CHUNK), CHUNK)

    def sib_copy(p):
        return remote(
            acc.at[p, other_rows], sib_buf.at[p], sib_ss.at[p], sib_rs.at[p], sibling
        )

    def rs_copy(p, d):
        to = lax.rem(z + d, NZ)
        rows = pl.ds(pl.multiple_of(to * CHUNK, CHUNK), CHUNK)
        return remote(
            mine.at[p, rows],
            rs_buf.at[p, d - 1],
            rs_ss.at[p, d - 1],
            rs_rs.at[p, d - 1],
            z_peer(d),
        )

    def za_copy(p, d):
        return remote(
            ci.at[p, chunk_rows],
            ci.at[p, chunk_rows],
            za_ss.at[p, d - 1],
            za_rs.at[p, d - 1],
            z_peer(d),
        )

    def swap_copy(p):
        return remote(
            ci.at[p, own_rows], ci.at[p, own_rows], sw_ss.at[p], sw_rs.at[p], sibling
        )

    def row_halo_copy(p):
        return remote(
            ci.at[p, pl.ds(0, DELAYS)],
            ci.at[p, pl.ds(STEPS, DELAYS)],
            rh_ss.at[p],
            rh_rs.at[p],
            plane_peer(NT - 1),
        )

    def forward_copy(p):
        return remote(
            ci.at[p, pl.ds(STEPS, DELAYS)],
            ci.at[p, pl.ds(STEPS, DELAYS)],
            fw_ss.at[p],
            fw_rs.at[p],
            sibling,
        )

    def scatter_copy(p):
        return remote(
            ci.at[p, chunk_rows],
            cj.at[p, chunk_rows],
            sc_ss.at[p],
            sc_rs.at[p],
            scatter_to,
        )

    def halo_scatter_copy(p):
        rows = pl.ds(
            pl.multiple_of(STEPS + lax.rem(chunk_at, 4) * CHUNK, CHUNK), CHUNK
        )
        return remote(
            ci.at[p, chunk_rows], cj.at[p, rows], hs_ss.at[p], hs_rs.at[p], halo_to
        )

    def ag_copy(p, d):
        return remote(
            cj.at[p, held_rows],
            cj.at[p, held_rows],
            ag_ss.at[p, d - 1],
            ag_rs.at[p, d - 1],
            plane_peer(d),
        )

    held_halo_rows = pl.ds(
        pl.multiple_of(STEPS + held_halo * CHUNK, CHUNK), CHUNK
    )

    def ag_halo_copy(p, d):
        return remote(
            cj.at[p, held_halo_rows],
            cj.at[p, held_halo_rows],
            ah_ss.at[p, d - 1],
            ah_rs.at[p, held_halo],
            plane_peer(d),
        )

    def start_rs(p):
        sib_copy(p).wait_recv()
        mine[p] = acc[p, own_rows] + sib_buf[p]
        for d in range(1, NZ):
            rs_copy(p, d).start()

    def finish_rs(p):
        total = mine[p, pl.ds(pl.multiple_of(z * CHUNK, CHUNK), CHUNK)]
        for d in range(1, NZ):
            rs_copy(p, d).wait_recv()
            total = total + rs_buf[p, d - 1]
        rounded = total.astype(jnp.bfloat16)
        ci[p, chunk_rows] = rounded

        @pl.when(scatter_self)
        def _():
            cj[p, chunk_rows] = rounded

        @pl.when(jnp.logical_not(scatter_self))
        def _():
            scatter_copy(p).start()

        @pl.when(halo_owner)
        def _():
            halo_scatter_copy(p).start()

        for d in range(1, NZ):
            za_copy(p, d).start()

    def start_ag(p):
        @pl.when(jnp.logical_not(scatter_self))
        def _():
            scatter_copy(p).wait_recv()

        for d in range(1, NT):
            ag_copy(p, d).start()

        @pl.when(holder)
        def _():
            halo_scatter_copy(p).wait_recv()
            for d in range(1, NT):
                ag_halo_copy(p, d).start()

    def finish_za(p):
        for d in range(1, NZ):
            za_copy(p, d).wait_recv()
        swap_copy(p).start()

        @pl.when(jnp.logical_and(core == 0, tm >= 1))
        def _():
            row_halo_copy(p).start()

    def finish_row_halo(p):
        @pl.when(jnp.logical_and(core == 0, tm < NT - 1))
        def _():
            row_halo_copy(p).wait_recv()
            forward_copy(p).start()

        @pl.when(jnp.logical_and(core == 1, tm < NT - 1))
        def _():
            forward_copy(p).wait_recv()

    def finish_ag(p):
        for d in range(1, NT):
            ag_copy(p, d).wait_recv()
        for k in range(4):

            @pl.when(
                jnp.logical_and(
                    has_next, jnp.logical_not(jnp.logical_and(holder, held_halo == k))
                )
            )
            def _():
                pltpu.make_async_copy(
                    cj.at[p, pl.ds(0, CHUNK)],
                    cj.at[p, pl.ds(STEPS + k * CHUNK, CHUNK)],
                    ah_rs.at[p, k],
                ).wait()

    def gram(p):
        return lax.dot_general(
            ci[p],
            cj[p],
            (((1,), (1,)), ((), ())),
            preferred_element_type=jnp.float32,
        )

    for k in range(KCUT):
        multiply(0, k)
    pl.semaphore_wait(barrier, expected)
    sib_copy(0).start()
    multiply(1, 0)
    multiply(1, 1)
    start_rs(0)
    multiply(1, 2)
    multiply(1, 3)
    sib_copy(1).start()
    start_rs(1)
    finish_rs(0)
    finish_rs(1)
    start_ag(0)
    finish_za(0)
    start_ag(1)
    finish_za(1)
    swap_copy(0).wait_recv()
    finish_row_halo(0)
    finish_ag(0)
    total = gram(0)
    swap_copy(1).wait_recv()
    finish_row_halo(1)
    finish_ag(1)
    total = total + gram(1)
    shift = 1
    while shift < DELAYS:
        moved = pltpu.roll(total, ROWS - shift, 0)
        total = total + pltpu.roll(moved, COLS - shift, 1)
        shift *= 2
    out[...] = total[:STEPS, :STEPS] * SCALE

    for p in range(PIECES):
        sib_copy(p).wait_send()
        swap_copy(p).wait_send()
        for d in range(1, NZ):
            rs_copy(p, d).wait_send()
            za_copy(p, d).wait_send()
        for d in range(1, NT):
            ag_copy(p, d).wait_send()

        @pl.when(holder)
        def _():
            for d in range(1, NT):
                ag_halo_copy(p, d).wait_send()

        @pl.when(jnp.logical_not(scatter_self))
        def _():
            scatter_copy(p).wait_send()

        @pl.when(halo_owner)
        def _():
            halo_scatter_copy(p).wait_send()

        @pl.when(jnp.logical_and(core == 0, tm >= 1))
        def _():
            row_halo_copy(p).wait_send()

        @pl.when(jnp.logical_and(core == 0, tm < NT - 1))
        def _():
            forward_copy(p).wait_send()


def per_device(snapshots, pod_basis):
    dma = pltpu.SemaphoreType.DMA
    pairs = [
        (PIECES,),
        (PIECES, NZ - 1),
        (PIECES, NZ - 1),
        (PIECES,),
        (PIECES,),
        (PIECES,),
        (PIECES,),
        (PIECES,),
        (PIECES, NT - 1),
    ]
    sems = [dma((KCUT,)), dma((PIECES, KCUT))]
    for shape in pairs:
        sems += [dma(shape), dma(shape)]
    sems += [dma((PIECES, NT - 1)), dma((PIECES, 4))]
    return pl.pallas_call(
        kernel,
        out_shape=jax.ShapeDtypeStruct((STEPS, STEPS), jnp.float32),
        in_specs=[pl.BlockSpec(memory_space=pl.ANY)] * 2,
        out_specs=pl.BlockSpec(memory_space=pltpu.VMEM),
        scratch_shapes=[
            pltpu.VMEM((POINTS, STEPS), jnp.bfloat16),
            pltpu.VMEM((PIECES, POINTS, HALF), jnp.bfloat16),
            pltpu.VMEM((PIECES, STEPS, HALF), jnp.float32),
            pltpu.VMEM((PIECES, OWN, HALF), jnp.float32),
            pltpu.VMEM((PIECES, OWN, HALF), jnp.float32),
            pltpu.VMEM((PIECES, NZ - 1, CHUNK, HALF), jnp.float32),
            pltpu.VMEM((PIECES, ROWS, HALF), jnp.bfloat16),
            pltpu.VMEM((PIECES, COLS, HALF), jnp.bfloat16),
        ]
        + sems,
        compiler_params=pltpu.CompilerParams(
            collective_id=0, has_side_effects=True, vmem_limit_bytes=40 << 20
        ),
    )(snapshots, pod_basis)


def solution(mesh):
    in_specs = (P("space", "tm"), P("space", None))
    out_specs = P("tm", "space")
    return jax.shard_map(
        per_device, mesh=mesh, in_specs=in_specs, out_specs=out_specs, check_vma=False
    )
```

time: 145 us -> 40.1 us (0.28)
  waiting for transfers between devices: 62.6 us -> 0 us
  blocking collectives: 54.6 us -> 0 us
  Pallas kernels: 0 us -> 33.7 us
  between operations: 13.4 us -> 0.01 us
  matrix products: 8.78 us -> 0 us
  local copies, waits for them, and re-layouts: 0 us -> 6.27 us
  other arithmetic: 5.43 us -> 0 us
    all_gather x1 -> x0, waiting for transfers between devices: 62.6 us -> none  [per_device(): all_coeffs = lax.all_gather(coeffs, 'tm', axis=1, tiled=True)]
    psum x1 -> x0, blocking collectives: 54.6 us -> none  [per_device(): coeffs = lax.psum(partial_value, 'space').astype(jnp.bfloat16)]
    pallas_call x0 -> x1, Pallas kernels: none -> 33.7 us  [per_device(): pl.pallas_call(kernel, out_shape=jax.ShapeDtypeStruct((STEPS, STEPS), jnp...]
    dot_general x2 -> x0, matrix products: 8.78 us -> none  [the longest x1 6.93 us: per_device(): jnp.dot(pod_basis.T, snapshots, preferred_element_type=jnp.float32)]
    unnamed x0 -> x5, local copies, waits for them, and re-layouts: none -> 6.27 us
    mul x1 -> x0, other arithmetic: 5.43 us -> none  [per_device(): return hankel_gram * (MODES * DELAYS) ** (-0.5)]
  transfers between devices with their start and end apart: 1 -> 0, of which waited for: 1 -> 0; matrix products, arithmetic and copies ran while one was open for 0% -> 0% of each run, Pallas kernels for 0% -> 0%
where the time goes in v1:
time: 40.1 us; the launch traced here: 40 us
  Pallas kernels  33.7 us (84%)
  local copies, waits for them, and re-layouts  6.27 us (16%)
    pallas_call x1, Pallas kernels, per_device(): pl.pallas_call(kernel, out_shape=jax.ShapeDtypeStruct((STEPS, STEPS), jnp...  33.7 us
    unnamed x5, local copies, waits for them, and re-layouts  6.27 us

profile of v1, /device:TPU:1, one launch (start us, length us, event | category | flops | bytes accessed | tf_op | source)
XLA Modules:
  0.0 40.0 jit_solution(1961745177029830868)
XLA Ops:
  0.0 0.0 copy-start
  0.0 3.4 %copy-done = bf16[8192,512]{1,0:T(8,128)(2,1)S(1)} copy-done((bf16[8192,512]{1,0:T(8,128)(2,1)S(1)}, bf16[8192,512]{1,0:T(8,128)(2,1)}, u32[]{:S(2)}) %copy-start) | copy-done | bytes 8388632
  3.4 0.0 copy-start.1
  3.4 2.2 %copy-done.1 = bf16[8192,256]{1,0:T(8,128)(2,1)S(1)} copy-done((bf16[8192,256]{1,0:T(8,128)(2,1)S(1)}, bf16[8192,256]{1,0:T(8,128)(2,1)}, u32[]{:S(2)}) %copy-start.1) | copy-done | bytes 4194328
  5.6 33.7 %shard_map.28 = f32[256,256]{1,0:T(8,128)S(1)} custom-call(bf16[8192,256]{1,0:T(8,128)(2,1)S(1)} %copy-done.1, bf16[8192,512]{1,0:T(8,128)(2,1)S(1)} %copy-done), custom_call_target="tpu_custom_call" | custom-call | tf_op jit(solution)/shard_map/pallas_call | solution.py:438
  39.3 0.7 %copy.4 = f32[256,256]{1,0:T(8,128)} copy(f32[256,256]{1,0:T(8,128)S(1)} %shard_map.28) | data formatting | bytes 524288
Async XLA Ops:
  0.0 3.4 %copy-start = (bf16[8192,512]{1,0:T(8,128)(2,1)S(1)}, bf16[8192,512]{1,0:T(8,128)(2,1)}, u32[]{:S(2)}) copy-start(bf16[8192,512]{1,0:T(8,128)(2,1)} %pod.1) | copy-start | bytes 25165828
  3.4 2.2 %copy-start.1 = (bf16[8192,256]{1,0:T(8,128)(2,1)S(1)}, bf16[8192,256]{1,0:T(8,128)(2,1)}, u32[]{:S(2)}) copy-start(bf16[8192,256]{1,0:T(8,128)(2,1)} %snap.1) | copy-start | bytes 12582916

commit v2 on v1

v2 whole, which is shorter than its diff:
```python
import jax
import jax.numpy as jnp
from jax import lax
from jax.experimental import pallas as pl
from jax.experimental.pallas import tpu as pltpu
from jax.sharding import PartitionSpec as P

MODES = 512
DELAYS = 64
MESH = pl.DeviceIdType.MESH
NZ = 8
NT = 16
SIDE = 4
STEPS = 256
POINTS = 8192
CHUNK = 16
OWN = STEPS // 2
KCUT = 8
KC = POINTS // KCUT
ROWS = STEPS + DELAYS
COLS = 384
PIECES = 2
WIDTH = MODES // PIECES
SCALE = (MODES * DELAYS) ** -0.5
ORDER = (4, 3, 5, 2, 6, 1, 7)
NARROW = (3, 4, 5)

PLACE = {
    (4, 0): (0, 0),
    (4, 1): (1, 0),
    (3, 0): (3, 0),
    (3, 1): (0, 1),
    (5, 0): (0, 3),
    (5, 1): (1, 1),
    (2, 0): (2, 0),
    (2, 1): (0, 2),
    (6, 0): (1, 3),
    (6, 1): (3, 1),
    (1, 0): (3, 3),
    (1, 1): (2, 1),
    (7, 0): (2, 3),
    (7, 1): (1, 2),
    (0, 0): (3, 2),
    (0, 1): (2, 2),
}
DX = [PLACE[r // 2, r % 2][0] for r in range(16)]
DY = [PLACE[r // 2, r % 2][1] for r in range(16)]
PLANE = sorted(
    ((dx, dy) for dx in range(SIDE) for dy in range(SIDE) if dx or dy),
    key=lambda o: -min(o[0], SIDE - o[0]) - min(o[1], SIDE - o[1]),
)
BACK = [0] * 16
for _r in range(16):
    BACK[DY[_r] * SIDE + DX[_r]] = _r


def lookup(table, index):
    value = jnp.int32(0)
    for at, entry in enumerate(table):
        value = value + jnp.where(index == at, entry, 0)
    return value


def kernel(
    snap,
    pod,
    out,
    sv,
    pv,
    acc,
    sib_buf,
    own,
    wide_out,
    wide_in,
    narrow_out,
    narrow_in,
    ci,
    cj,
    s_sem,
    p_sem,
    sib_ss,
    sib_rs,
    rs_ss,
    rs_rs,
    za_ss,
    za_rs,
    sw_ss,
    sw_rs,
    rh_ss,
    rh_rs,
    sc_ss,
    sc_rs,
    hs_ss,
    hs_rs,
    ag_ss,
    ag_rs,
    ah_ss,
    ah_rs,
):
    space = lax.axis_index("space")
    tm = lax.axis_index("tm")
    z = space // 2
    core = lax.rem(space, 2)
    x = lax.rem(tm, SIDE)
    y = tm // SIDE
    chunk_at = core * NZ + z

    sibling = {"space": z * 2 + 1 - core, "tm": tm}

    def z_peer(d):
        return {"space": lax.rem(z + d, NZ) * 2 + core, "tm": tm}

    def plane_peer(d):
        dx, dy = PLANE[d]
        return {"space": space, "tm": lax.rem(y + dy, SIDE) * SIDE + lax.rem(x + dx, SIDE)}

    rank = lax.rem(z - tm // 2 + NZ, NZ) * 2 + core
    to_x = lax.rem(x + lookup(DX, rank), SIDE)
    to_y = lax.rem(y + lookup(DY, rank), SIDE)
    scatter_to = {"space": tm, "tm": to_y * SIDE + to_x}
    off_x = lax.rem(x - lax.rem(space, SIDE) + SIDE, SIDE)
    off_y = lax.rem(y - space // SIDE + SIDE, SIDE)
    from_rank = lookup(BACK, off_y * SIDE + off_x)
    from_z = lax.rem(z + from_rank // 2, NZ)
    from_core = lax.rem(from_rank, 2)
    held = from_core * NZ + from_z
    scatter_from = {"space": from_z * 2 + from_core, "tm": space}

    halo_owner = jnp.logical_and(chunk_at < 4, tm >= 1)
    halo_plane = lax.rem(tm + NT - 1, NT)
    halo_turn = lax.rem(lax.rem(z - halo_plane // 2 + NZ, SIDE) + 1, SIDE)
    halo_to = {"space": halo_plane, "tm": lax.rem(y + halo_turn, SIDE) * SIDE + x}
    has_next = space < NT - 1
    next_block = lax.rem(space + 1, NT)
    holder = jnp.logical_and(has_next, x == lax.rem(next_block, SIDE))
    held_turn = lax.rem(y - next_block // SIDE - 1 + 2 * SIDE, SIDE)
    held_halo = lax.rem(held_turn + z, SIDE)
    halo_from = {"space": held_halo * 2, "tm": next_block}

    sends_row_halo = jnp.logical_and(core == 0, tm >= 1)
    takes_row_halo = tm < NT - 1
    before = lax.rem(tm + NT - 1, NT)
    after = lax.rem(tm + 1, NT)

    def snap_copy(k):
        at = pl.ds(k * KC, KC)
        return pltpu.make_async_copy(snap.at[at], sv.at[at], s_sem.at[k])

    def pod_copy(k):
        at = pl.ds(k * KC, KC)
        return pltpu.make_async_copy(pod.at[at], pv.at[at], p_sem.at[k])

    for k in range(KCUT):
        snap_copy(k).start()
        pod_copy(k).start()

    barrier = pltpu.get_barrier_semaphore()

    def greet(who):
        pl.semaphore_signal(barrier, inc=1, device_id=who, device_id_type=MESH)

    greet(sibling)
    for d in range(1, NZ):
        greet(z_peer(d))
    for d in range(NT - 1):
        greet(plane_peer(d))
    greet(scatter_from)

    @pl.when(holder)
    def _():
        greet(halo_from)

    @pl.when(jnp.logical_and(core == 1, takes_row_halo))
    def _():
        greet({"space": z * 2, "tm": after})

    expected = (
        1
        + (NZ - 1)
        + (NT - 1)
        + 1
        + jnp.where(halo_owner, 1, 0)
        + jnp.where(sends_row_halo, 1, 0)
    )

    cj[:, ROWS:, :] = jnp.zeros((PIECES, COLS - ROWS, WIDTH), jnp.bfloat16)

    @pl.when(jnp.logical_not(has_next))
    def _():
        cj[:, STEPS:ROWS, :] = jnp.zeros((PIECES, DELAYS, WIDTH), jnp.bfloat16)

    @pl.when(jnp.logical_not(takes_row_halo))
    def _():
        ci[:, STEPS:ROWS, :] = jnp.zeros((PIECES, DELAYS, WIDTH), jnp.bfloat16)

    def remote(src, dst, ss, rs, who):
        return pltpu.make_async_remote_copy(
            src_ref=src,
            dst_ref=dst,
            send_sem=ss,
            recv_sem=rs,
            device_id=who,
            device_id_type=MESH,
        )

    def rows_of(start, size):
        return pl.ds(pl.multiple_of(start, CHUNK), size)

    chunk_rows = rows_of(chunk_at * CHUNK, CHUNK)
    held_rows = rows_of(held * CHUNK, CHUNK)
    held_halo_rows = rows_of(STEPS + held_halo * CHUNK, CHUNK)
    own_rows = rows_of(core * OWN, OWN)

    def sib_copy(p, d):
        to = lax.rem(z + d, NZ)
        return remote(
            acc.at[p, rows_of((1 - core) * OWN + to * CHUNK, CHUNK)],
            sib_buf.at[p, d],
            sib_ss.at[p, d],
            sib_rs.at[p, d],
            sibling,
        )

    def rs_copy(p, d):
        out_buf, in_buf = (
            (narrow_out, narrow_in) if d in NARROW else (wide_out, wide_in)
        )
        return remote(
            out_buf.at[p, d - 1],
            in_buf.at[p, d - 1],
            rs_ss.at[p, d - 1],
            rs_rs.at[p, d - 1],
            z_peer(d),
        )

    def za_copy(p, d):
        return remote(
            ci.at[p, chunk_rows],
            ci.at[p, chunk_rows],
            za_ss.at[p, d - 1],
            za_rs.at[p, d - 1],
            z_peer(d),
        )

    def swap_copy(p):
        return remote(
            ci.at[p, own_rows], ci.at[p, own_rows], sw_ss.at[p], sw_rs.at[p], sibling
        )

    def row_halo_copy(p, c):
        return remote(
            ci.at[p, pl.ds(0, DELAYS)],
            ci.at[p, pl.ds(STEPS, DELAYS)],
            rh_ss.at[p, c],
            rh_rs.at[p],
            {"space": z * 2 + c, "tm": before},
        )

    def scatter_copy(p):
        return remote(
            ci.at[p, chunk_rows],
            cj.at[p, chunk_rows],
            sc_ss.at[p],
            sc_rs.at[p],
            scatter_to,
        )

    def halo_scatter_copy(p):
        rows = rows_of(STEPS + lax.rem(z, SIDE) * CHUNK, CHUNK)
        return remote(
            ci.at[p, chunk_rows], cj.at[p, rows], hs_ss.at[p], hs_rs.at[p], halo_to
        )

    def ag_copy(p, d):
        return remote(
            cj.at[p, held_rows],
            cj.at[p, held_rows],
            ag_ss.at[p, d],
            ag_rs.at[p, d],
            plane_peer(d),
        )

    def ag_halo_copy(p, d):
        return remote(
            cj.at[p, held_halo_rows],
            cj.at[p, held_halo_rows],
            ah_ss.at[p, d],
            ah_rs.at[p, held_halo],
            plane_peer(d),
        )

    def start_sum(p):
        for d in ORDER + (0,):
            sib_copy(p, d).wait_recv()
            to = lax.rem(z + d, NZ)
            both = acc[p, rows_of(core * OWN + to * CHUNK, CHUNK)] + sib_buf[p, d]
            if d == 0:
                own[p] = both
            elif d in NARROW:
                narrow_out[p, d - 1] = both.astype(jnp.bfloat16)
            else:
                wide_out[p, d - 1] = both
            if d > 0:
                rs_copy(p, d).start()

    def finish_sum(p):
        total = own[p]
        for d in ORDER[::-1]:
            rs_copy(p, d).wait_recv()
            in_buf = narrow_in if d in NARROW else wide_in
            total = total + in_buf[p, d - 1].astype(jnp.float32)
        ci[p, chunk_rows] = total.astype(jnp.bfloat16)
        scatter_copy(p).start()

        @pl.when(halo_owner)
        def _():
            halo_scatter_copy(p).start()

        for d in ORDER:
            za_copy(p, d).start()

    def start_plane(p):
        scatter_copy(p).wait_recv()
        for d in range(NT - 1):
            ag_copy(p, d).start()

        @pl.when(holder)
        def _():
            halo_scatter_copy(p).wait_recv()
            for d in range(NT - 1):
                ag_halo_copy(p, d).start()

    def finish_z(p):
        for d in ORDER[::-1]:
            za_copy(p, d).wait_recv()
        swap_copy(p).start()

        @pl.when(sends_row_halo)
        def _():
            row_halo_copy(p, 0).start()
            row_halo_copy(p, 1).start()

    def gram(p):
        swap_copy(p).wait_recv()

        @pl.when(takes_row_halo)
        def _():
            row_halo_copy(p, 0).wait_recv()

        for d in range(NT - 1)[::-1]:
            ag_copy(p, d).wait_recv()
        for k in range(4):

            @pl.when(
                jnp.logical_and(
                    has_next, jnp.logical_not(jnp.logical_and(holder, held_halo == k))
                )
            )
            def _():
                pltpu.make_async_copy(
                    cj.at[p, pl.ds(0, CHUNK)],
                    cj.at[p, pl.ds(STEPS + k * CHUNK, CHUNK)],
                    ah_rs.at[p, k],
                ).wait()

        return lax.dot_general(
            ci[p],
            cj[p],
            (((1,), (1,)), ((), ())),
            preferred_element_type=jnp.float32,
        )

    for k in range(KCUT):
        snap_copy(k).wait()
        pod_copy(k).wait()
        at = pl.ds(k * KC, KC)
        term = lax.dot_general(
            sv[at],
            pv[at],
            (((0,), (0,)), ((), ())),
            preferred_element_type=jnp.float32,
        )
        for p in range(PIECES):
            part = term[:, p * WIDTH : (p + 1) * WIDTH]
            if k == 0:
                acc[p] = part
            else:
                acc[p] += part

    pl.semaphore_wait(barrier, expected)

    for p in range(PIECES):
        for d in ORDER + (0,):
            sib_copy(p, d).start()
    for p in range(PIECES):
        start_sum(p)
    for p in range(PIECES):
        finish_sum(p)
    for p in range(PIECES):
        start_plane(p)
        finish_z(p)

    for p in range(PIECES):
        for d in range(NZ):
            sib_copy(p, d).wait_send()
        for d in range(1, NZ):
            rs_copy(p, d).wait_send()
            za_copy(p, d).wait_send()
        scatter_copy(p).wait_send()

        @pl.when(halo_owner)
        def _():
            halo_scatter_copy(p).wait_send()

    window = gram(0)
    for p in range(1, PIECES):
        window = window + gram(p)
    shift = 1
    while shift < DELAYS:
        moved = pltpu.roll(window, ROWS - shift, 0)
        window = window + pltpu.roll(moved, COLS - shift, 1)
        shift *= 2
    out[...] = window[:STEPS, :STEPS] * SCALE

    for p in range(PIECES):
        swap_copy(p).wait_send()

        @pl.when(sends_row_halo)
        def _():
            row_halo_copy(p, 0).wait_send()
            row_halo_copy(p, 1).wait_send()

        for d in range(NT - 1):
            ag_copy(p, d).wait_send()

        @pl.when(holder)
        def _():
            for d in range(NT - 1):
                ag_halo_copy(p, d).wait_send()


def per_device(snapshots, pod_basis):
    dma = pltpu.SemaphoreType.DMA
    f32, bf16 = jnp.float32, jnp.bfloat16
    sems = [dma((KCUT,)), dma((KCUT,))]
    for sent, received in (
        ((NZ,), (NZ,)),
        ((NZ - 1,), (NZ - 1,)),
        ((NZ - 1,), (NZ - 1,)),
        ((), ()),
        ((2,), ()),
        ((), ()),
        ((), ()),
        ((NT - 1,), (NT - 1,)),
        ((NT - 1,), (4,)),
    ):
        sems += [dma((PIECES,) + sent), dma((PIECES,) + received)]
    return pl.pallas_call(
        kernel,
        out_shape=jax.ShapeDtypeStruct((STEPS, STEPS), f32),
        in_specs=[pl.BlockSpec(memory_space=pl.ANY)] * 2,
        out_specs=pl.BlockSpec(memory_space=pltpu.VMEM),
        scratch_shapes=[
            pltpu.VMEM((POINTS, STEPS), bf16),
            pltpu.VMEM((POINTS, MODES), bf16),
            pltpu.VMEM((PIECES, STEPS, WIDTH), f32),
            pltpu.VMEM((PIECES, NZ, CHUNK, WIDTH), f32),
            pltpu.VMEM((PIECES, CHUNK, WIDTH), f32),
            pltpu.VMEM((PIECES, NZ - 1, CHUNK, WIDTH), f32),
            pltpu.VMEM((PIECES, NZ - 1, CHUNK, WIDTH), f32),
            pltpu.VMEM((PIECES, NZ - 1, CHUNK, WIDTH), bf16),
            pltpu.VMEM((PIECES, NZ - 1, CHUNK, WIDTH), bf16),
            pltpu.VMEM((PIECES, ROWS, WIDTH), bf16),
            pltpu.VMEM((PIECES, COLS, WIDTH), bf16),
        ]
        + sems,
        compiler_params=pltpu.CompilerParams(
            collective_id=0, has_side_effects=True, vmem_limit_bytes=62 << 20
        ),
    )(snapshots, pod_basis)


def solution(mesh):
    in_specs = (P("space", "tm"), P("space", None))
    out_specs = P("tm", "space")
    return jax.shard_map(
        per_device, mesh=mesh, in_specs=in_specs, out_specs=out_specs, check_vma=False
    )
```

time: 40.1 us -> 34.4 us (0.86)
  local copies, waits for them, and re-layouts: 6.27 us -> 1.67 us
  Pallas kernels: 33.7 us -> 32.7 us
    unnamed x5 -> x1, local copies, waits for them, and re-layouts: 6.27 us -> 1.67 us
    pallas_call x1, Pallas kernels: 33.7 us -> 32.7 us  [per_device(): pl.pallas_call(kernel, out_shape=jax.ShapeDtypeStruct((STEPS, STEPS), f32...]
where the time goes in v2:
time: 34.4 us; the launch traced here: 34.3 us
  Pallas kernels  32.7 us (95%)
  local copies, waits for them, and re-layouts  1.67 us (5%)
    pallas_call x1, Pallas kernels, per_device(): pl.pallas_call(kernel, out_shape=jax.ShapeDtypeStruct((STEPS, STEPS), f32...  32.7 us
    unnamed x1, local copies, waits for them, and re-layouts  1.67 us

profile of v2, /device:TPU:1, one launch (start us, length us, event | category | flops | bytes accessed | tf_op | source)
XLA Modules:
  0.0 34.3 jit_solution(8899707791693388642)
XLA Ops:
  0.0 32.7 %shard_map.28 = f32[256,256]{1,0:T(8,128)} custom-call(bf16[8192,256]{1,0:T(8,128)(2,1)} %snap.1, bf16[8192,512]{1,0:T(8,128)(2,1)} %pod.1), custom_call_target="tpu_custom_call" | custom-call | tf_op jit(solution)/shard_map/pallas_call | solution.py:458
  32.7 1.7 %copy.4 = f32[256,256]{1,0:T(8,128)} copy(f32[256,256]{1,0:T(8,128)} %shard_map.28) | data formatting | bytes 524288

commit v3 on v2

--- a/solution.py
+++ b/solution.py
@@ -14,16 +14,18 @@
 STEPS = 256
 POINTS = 8192
 CHUNK = 16
+HALO = DELAYS // CHUNK
 OWN = STEPS // 2
-KCUT = 8
+KCUT = 4
 KC = POINTS // KCUT
+SEND_AFTER = 2
 ROWS = STEPS + DELAYS
 COLS = 384
 PIECES = 2
 WIDTH = MODES // PIECES
 SCALE = (MODES * DELAYS) ** -0.5
 ORDER = (4, 3, 5, 2, 6, 1, 7)
-NARROW = (3, 4, 5)
+NARROW = (2, 3, 4, 5, 6)
 
 PLACE = {
     (4, 0): (0, 0),
@@ -69,7 +71,6 @@
     pv,
     acc,
     sib_buf,
-    own,
     wide_out,
     wide_in,
     narrow_out,
@@ -88,6 +89,8 @@
     sw_rs,
     rh_ss,
     rh_rs,
+    fw_ss,
+    fw_rs,
     sc_ss,
     sc_rs,
     hs_ss,
@@ -97,13 +100,33 @@
     ah_ss,
     ah_rs,
 ):
+    def snap_copy(k):
+        at = pl.ds(k * KC, KC)
+        return pltpu.make_async_copy(snap.at[at], sv.at[at], s_sem.at[k])
+
+    def pod_copy(p, k):
+        at = pl.ds(k * KC, KC)
+        wide = pl.ds(p * WIDTH, WIDTH)
+        return pltpu.make_async_copy(pod.at[at, wide], pv.at[p, at], p_sem.at[p, k])
+
+    for k in range(KCUT):
+        snap_copy(k).start()
+        pod_copy(0, k).start()
+    for p in range(1, PIECES):
+        for k in range(KCUT):
+            pod_copy(p, k).start()
+
     space = lax.axis_index("space")
     tm = lax.axis_index("tm")
     z = space // 2
     core = lax.rem(space, 2)
     x = lax.rem(tm, SIDE)
     y = tm // SIDE
-    chunk_at = core * NZ + z
+    def turn_of(at):
+        return at // 2 + lax.rem(at, 2) * (NZ // 2)
+
+    turn = turn_of(z)
+    chunk_at = core * NZ + turn
 
     sibling = {"space": z * 2 + 1 - core, "tm": tm}
 
@@ -123,36 +146,23 @@
     from_rank = lookup(BACK, off_y * SIDE + off_x)
     from_z = lax.rem(z + from_rank // 2, NZ)
     from_core = lax.rem(from_rank, 2)
-    held = from_core * NZ + from_z
+    held = from_core * NZ + turn_of(from_z)
     scatter_from = {"space": from_z * 2 + from_core, "tm": space}
 
-    halo_owner = jnp.logical_and(chunk_at < 4, tm >= 1)
+    halo_owner = jnp.logical_and(chunk_at < HALO, tm >= 1)
     halo_plane = lax.rem(tm + NT - 1, NT)
-    halo_turn = lax.rem(lax.rem(z - halo_plane // 2 + NZ, SIDE) + 1, SIDE)
+    halo_turn = lax.rem(lax.rem(z - halo_plane // 2 + NZ, NZ) // 2 + 2, SIDE)
     halo_to = {"space": halo_plane, "tm": lax.rem(y + halo_turn, SIDE) * SIDE + x}
     has_next = space < NT - 1
     next_block = lax.rem(space + 1, NT)
     holder = jnp.logical_and(has_next, x == lax.rem(next_block, SIDE))
-    held_turn = lax.rem(y - next_block // SIDE - 1 + 2 * SIDE, SIDE)
-    held_halo = lax.rem(held_turn + z, SIDE)
-    halo_from = {"space": held_halo * 2, "tm": next_block}
-
-    sends_row_halo = jnp.logical_and(core == 0, tm >= 1)
+    held_turn = lax.rem(y - next_block // SIDE + 2 + SIDE, SIDE)
+    held_halo = lax.rem(z + lax.rem(z, 2) + held_turn * 2, NZ) // 2
+    halo_from = {"space": held_halo * 4, "tm": next_block}
+
     takes_row_halo = tm < NT - 1
     before = lax.rem(tm + NT - 1, NT)
     after = lax.rem(tm + 1, NT)
-
-    def snap_copy(k):
-        at = pl.ds(k * KC, KC)
-        return pltpu.make_async_copy(snap.at[at], sv.at[at], s_sem.at[k])
-
-    def pod_copy(k):
-        at = pl.ds(k * KC, KC)
-        return pltpu.make_async_copy(pod.at[at], pv.at[at], p_sem.at[k])
-
-    for k in range(KCUT):
-        snap_copy(k).start()
-        pod_copy(k).start()
 
     barrier = pltpu.get_barrier_semaphore()
 
@@ -170,17 +180,17 @@
     def _():
         greet(halo_from)
 
-    @pl.when(jnp.logical_and(core == 1, takes_row_halo))
+    @pl.when(jnp.logical_and(core == 0, takes_row_halo))
     def _():
-        greet({"space": z * 2, "tm": after})
+        for k in range(HALO):
+            greet({"space": k * 4, "tm": after})
 
     expected = (
         1
         + (NZ - 1)
         + (NT - 1)
         + 1
-        + jnp.where(halo_owner, 1, 0)
-        + jnp.where(sends_row_halo, 1, 0)
+        + jnp.where(halo_owner, 1 + NZ, 0)
     )
 
     cj[:, ROWS:, :] = jnp.zeros((PIECES, COLS - ROWS, WIDTH), jnp.bfloat16)
@@ -210,14 +220,14 @@
     held_rows = rows_of(held * CHUNK, CHUNK)
     held_halo_rows = rows_of(STEPS + held_halo * CHUNK, CHUNK)
     own_rows = rows_of(core * OWN, OWN)
-
-    def sib_copy(p, d):
-        to = lax.rem(z + d, NZ)
-        return remote(
-            acc.at[p, rows_of((1 - core) * OWN + to * CHUNK, CHUNK)],
-            sib_buf.at[p, d],
-            sib_ss.at[p, d],
-            sib_rs.at[p, d],
+    halo_rows = rows_of(STEPS + lax.rem(turn, HALO) * CHUNK, CHUNK)
+
+    def sib_copy(p):
+        return remote(
+            acc.at[p, rows_of((1 - core) * OWN, OWN)],
+            sib_buf.at[p],
+            sib_ss.at[p],
+            sib_rs.at[p],
             sibling,
         )
 
@@ -226,7 +236,7 @@
             (narrow_out, narrow_in) if d in NARROW else (wide_out, wide_in)
         )
         return remote(
-            out_buf.at[p, d - 1],
+            out_buf.at[p, rows_of(turn_of(lax.rem(z + d, NZ)) * CHUNK, CHUNK)],
             in_buf.at[p, d - 1],
             rs_ss.at[p, d - 1],
             rs_rs.at[p, d - 1],
@@ -247,13 +257,23 @@
             ci.at[p, own_rows], ci.at[p, own_rows], sw_ss.at[p], sw_rs.at[p], sibling
         )
 
-    def row_halo_copy(p, c):
-        return remote(
-            ci.at[p, pl.ds(0, DELAYS)],
-            ci.at[p, pl.ds(STEPS, DELAYS)],
-            rh_ss.at[p, c],
-            rh_rs.at[p],
-            {"space": z * 2 + c, "tm": before},
+    def row_halo_copy(p, d):
+        return remote(
+            ci.at[p, chunk_rows],
+            ci.at[p, halo_rows],
+            rh_ss.at[p, d],
+            rh_rs.at[p, lax.rem(turn, HALO)],
+            {"space": lax.rem(z + d, NZ) * 2, "tm": before},
+        )
+
+    def row_halo_arrival(p, k):
+        at = pl.ds(STEPS + k * CHUNK, CHUNK)
+        return pltpu.make_async_copy(ci.at[p, at], ci.at[p, at], rh_rs.at[p, k])
+
+    def forward_copy(p):
+        at = pl.ds(STEPS, DELAYS)
+        return remote(
+            ci.at[p, at], ci.at[p, at], fw_ss.at[p], fw_rs.at[p], sibling
         )
 
     def scatter_copy(p):
@@ -266,9 +286,8 @@
         )
 
     def halo_scatter_copy(p):
-        rows = rows_of(STEPS + lax.rem(z, SIDE) * CHUNK, CHUNK)
-        return remote(
-            ci.at[p, chunk_rows], cj.at[p, rows], hs_ss.at[p], hs_rs.at[p], halo_to
+        return remote(
+            ci.at[p, chunk_rows], cj.at[p, halo_rows], hs_ss.at[p], hs_rs.at[p], halo_to
         )
 
     def ag_copy(p, d):
@@ -290,21 +309,15 @@
         )
 
     def start_sum(p):
-        for d in ORDER + (0,):
-            sib_copy(p, d).wait_recv()
-            to = lax.rem(z + d, NZ)
-            both = acc[p, rows_of(core * OWN + to * CHUNK, CHUNK)] + sib_buf[p, d]
-            if d == 0:
-                own[p] = both
-            elif d in NARROW:
-                narrow_out[p, d - 1] = both.astype(jnp.bfloat16)
-            else:
-                wide_out[p, d - 1] = both
-            if d > 0:
-                rs_copy(p, d).start()
+        sib_copy(p).wait_recv()
+        both = acc[p, own_rows] + sib_buf[p]
+        wide_out[p] = both
+        narrow_out[p] = both.astype(jnp.bfloat16)
+        for d in ORDER:
+            rs_copy(p, d).start()
 
     def finish_sum(p):
-        total = own[p]
+        total = wide_out[p, rows_of(turn * CHUNK, CHUNK)]
         for d in ORDER[::-1]:
             rs_copy(p, d).wait_recv()
             in_buf = narrow_in if d in NARROW else wide_in
@@ -316,14 +329,21 @@
         def _():
             halo_scatter_copy(p).start()
 
+    def start_z(p):
         for d in ORDER:
             za_copy(p, d).start()
+
+        @pl.when(halo_owner)
+        def _():
+            for d in ORDER + (0,):
+                row_halo_copy(p, d).start()
 
     def start_plane(p):
         scatter_copy(p).wait_recv()
         for d in range(NT - 1):
             ag_copy(p, d).start()
 
+    def start_halo(p):
         @pl.when(holder)
         def _():
             halo_scatter_copy(p).wait_recv()
@@ -335,21 +355,22 @@
             za_copy(p, d).wait_recv()
         swap_copy(p).start()
 
-        @pl.when(sends_row_halo)
-        def _():
-            row_halo_copy(p, 0).start()
-            row_halo_copy(p, 1).start()
+        @pl.when(jnp.logical_and(core == 0, takes_row_halo))
+        def _():
+            for k in range(HALO):
+                row_halo_arrival(p, k).wait()
+            forward_copy(p).start()
 
     def gram(p):
         swap_copy(p).wait_recv()
 
-        @pl.when(takes_row_halo)
-        def _():
-            row_halo_copy(p, 0).wait_recv()
+        @pl.when(jnp.logical_and(core == 1, takes_row_halo))
+        def _():
+            forward_copy(p).wait_recv()
 
         for d in range(NT - 1)[::-1]:
             ag_copy(p, d).wait_recv()
-        for k in range(4):
+        for k in range(HALO):
 
             @pl.when(
                 jnp.logical_and(
@@ -370,39 +391,46 @@
             preferred_element_type=jnp.float32,
         )
 
+    def multiply(p, k):
+        if p == 0:
+            snap_copy(k).wait()
+        pod_copy(p, k).wait()
+        at = pl.ds(k * KC, KC)
+        for part in range(2):
+            rows = slice(part * OWN, (part + 1) * OWN)
+            term = lax.dot_general(
+                sv[at, rows],
+                pv[p, at],
+                (((0,), (0,)), ((), ())),
+                preferred_element_type=jnp.float32,
+            )
+            if k == 0:
+                acc[p, rows] = term
+            else:
+                acc[p, rows] += term
+
     for k in range(KCUT):
-        snap_copy(k).wait()
-        pod_copy(k).wait()
-        at = pl.ds(k * KC, KC)
-        term = lax.dot_general(
-            sv[at],
-            pv[at],
-            (((0,), (0,)), ((), ())),
-            preferred_element_type=jnp.float32,
-        )
-        for p in range(PIECES):
-            part = term[:, p * WIDTH : (p + 1) * WIDTH]
-            if k == 0:
-                acc[p] = part
-            else:
-                acc[p] += part
-
+        multiply(0, k)
     pl.semaphore_wait(barrier, expected)
-
-    for p in range(PIECES):
-        for d in ORDER + (0,):
-            sib_copy(p, d).start()
-    for p in range(PIECES):
-        start_sum(p)
+    sib_copy(0).start()
+    for k in range(KCUT):
+        if k == SEND_AFTER:
+            start_sum(0)
+        multiply(1, k)
+    sib_copy(1).start()
+    start_sum(1)
     for p in range(PIECES):
         finish_sum(p)
     for p in range(PIECES):
+        start_z(p)
+    for p in range(PIECES):
         start_plane(p)
+        start_halo(p)
+    for p in range(PIECES):
         finish_z(p)
 
     for p in range(PIECES):
-        for d in range(NZ):
-            sib_copy(p, d).wait_send()
+        sib_copy(p).wait_send()
         for d in range(1, NZ):
             rs_copy(p, d).wait_send()
             za_copy(p, d).wait_send()
@@ -411,6 +439,8 @@
         @pl.when(halo_owner)
         def _():
             halo_scatter_copy(p).wait_send()
+            for d in range(NZ):
+                row_halo_copy(p, d).wait_send()
 
     window = gram(0)
     for p in range(1, PIECES):
@@ -425,10 +455,9 @@
     for p in range(PIECES):
         swap_copy(p).wait_send()
 
-        @pl.when(sends_row_halo)
-        def _():
-            row_halo_copy(p, 0).wait_send()
-            row_halo_copy(p, 1).wait_send()
+        @pl.when(jnp.logical_and(core == 0, takes_row_halo))
+        def _():
+            forward_copy(p).wait_send()
 
         for d in range(NT - 1):
             ag_copy(p, d).wait_send()
@@ -442,13 +471,14 @@
 def per_device(snapshots, pod_basis):
     dma = pltpu.SemaphoreType.DMA
     f32, bf16 = jnp.float32, jnp.bfloat16
-    sems = [dma((KCUT,)), dma((KCUT,))]
+    sems = [dma((KCUT,)), dma((PIECES, KCUT))]
     for sent, received in (
-        ((NZ,), (NZ,)),
+        ((), ()),
         ((NZ - 1,), (NZ - 1,)),
         ((NZ - 1,), (NZ - 1,)),
         ((), ()),
-        ((2,), ()),
+        ((NZ,), (HALO,)),
+        ((), ()),
         ((), ()),
         ((), ()),
         ((NT - 1,), (NT - 1,)),
@@ -462,20 +492,19 @@
         out_specs=pl.BlockSpec(memory_space=pltpu.VMEM),
         scratch_shapes=[
             pltpu.VMEM((POINTS, STEPS), bf16),
-            pltpu.VMEM((POINTS, MODES), bf16),
+            pltpu.VMEM((PIECES, POINTS, WIDTH), bf16),
             pltpu.VMEM((PIECES, STEPS, WIDTH), f32),
-            pltpu.VMEM((PIECES, NZ, CHUNK, WIDTH), f32),
-            pltpu.VMEM((PIECES, CHUNK, WIDTH), f32),
+            pltpu.VMEM((PIECES, OWN, WIDTH), f32),
+            pltpu.VMEM((PIECES, OWN, WIDTH), f32),
             pltpu.VMEM((PIECES, NZ - 1, CHUNK, WIDTH), f32),
-            pltpu.VMEM((PIECES, NZ - 1, CHUNK, WIDTH), f32),
-            pltpu.VMEM((PIECES, NZ - 1, CHUNK, WIDTH), bf16),
+            pltpu.VMEM((PIECES, OWN, WIDTH), bf16),
             pltpu.VMEM((PIECES, NZ - 1, CHUNK, WIDTH), bf16),
             pltpu.VMEM((PIECES, ROWS, WIDTH), bf16),
             pltpu.VMEM((PIECES, COLS, WIDTH), bf16),
         ]
         + sems,
         compiler_params=pltpu.CompilerParams(
-            collective_id=0, has_side_effects=True, vmem_limit_bytes=62 << 20
+            collective_id=0, has_side_effects=True, vmem_limit_bytes=50 << 20
         ),
     )(snapshots, pod_basis)
 

time: 34.4 us -> 31.6 us (0.919)
  Pallas kernels: 32.7 us -> 30.9 us
  local copies, waits for them, and re-layouts: 1.67 us -> 0.71 us
    pallas_call x1, Pallas kernels: 32.7 us -> 30.9 us  [per_device(): pl.pallas_call(kernel, out_shape=jax.ShapeDtypeStruct((STEPS, STEPS), f32...]
    unnamed x1, local copies, waits for them, and re-layouts: 1.67 us -> 0.71 us
where the time goes in v3:
time: 31.6 us
  Pallas kernels  30.9 us (98%)
  local copies, waits for them, and re-layouts  0.71 us (2%)
    pallas_call x1, Pallas kernels, per_device(): pl.pallas_call(kernel, out_shape=jax.ShapeDtypeStruct((STEPS, STEPS), f32...  30.9 us
    unnamed x1, local copies, waits for them, and re-layouts  0.71 us

profile of v3, /device:TPU:1, one launch (start us, length us, event | category | flops | bytes accessed | tf_op | source)
XLA Modules:
  0.0 31.6 jit_solution(8240805056970670370)
XLA Ops:
  0.0 30.9 %shard_map.28 = f32[256,256]{1,0:T(8,128)S(1)} custom-call(bf16[8192,256]{1,0:T(8,128)(2,1)} %snap.1, bf16[8192,512]{1,0:T(8,128)(2,1)} %pod.1), custom_call_target="tpu_custom_call" | custom-call | tf_op jit(solution)/shard_map/pallas_call | solution.py:488
  30.9 0.7 %copy.4 = f32[256,256]{1,0:T(8,128)} copy(f32[256,256]{1,0:T(8,128)S(1)} %shard_map.28) | data formatting | bytes 524288

commit v4 on v3

--- a/solution.py
+++ b/solution.py
@@ -18,7 +18,7 @@
 OWN = STEPS // 2
 KCUT = 4
 KC = POINTS // KCUT
-SEND_AFTER = 2
+SEND_AFTER = 1
 ROWS = STEPS + DELAYS
 COLS = 384
 PIECES = 2
@@ -201,7 +201,7 @@
 
     @pl.when(jnp.logical_not(takes_row_halo))
     def _():
-        ci[:, STEPS:ROWS, :] = jnp.zeros((PIECES, DELAYS, WIDTH), jnp.bfloat16)
+        ci[STEPS:ROWS, :] = jnp.zeros((DELAYS, MODES), jnp.bfloat16)
 
     def remote(src, dst, ss, rs, who):
         return pltpu.make_async_remote_copy(
@@ -216,6 +216,9 @@
     def rows_of(start, size):
         return pl.ds(pl.multiple_of(start, CHUNK), size)
 
+    def wide_of(p):
+        return pl.ds(p * WIDTH, WIDTH)
+
     chunk_rows = rows_of(chunk_at * CHUNK, CHUNK)
     held_rows = rows_of(held * CHUNK, CHUNK)
     held_halo_rows = rows_of(STEPS + held_halo * CHUNK, CHUNK)
@@ -243,42 +246,42 @@
             z_peer(d),
         )
 
-    def za_copy(p, d):
-        return remote(
-            ci.at[p, chunk_rows],
-            ci.at[p, chunk_rows],
-            za_ss.at[p, d - 1],
-            za_rs.at[p, d - 1],
+    def za_copy(d):
+        return remote(
+            ci.at[chunk_rows],
+            ci.at[chunk_rows],
+            za_ss.at[d - 1],
+            za_rs.at[d - 1],
             z_peer(d),
         )
 
-    def swap_copy(p):
-        return remote(
-            ci.at[p, own_rows], ci.at[p, own_rows], sw_ss.at[p], sw_rs.at[p], sibling
-        )
-
-    def row_halo_copy(p, d):
-        return remote(
-            ci.at[p, chunk_rows],
-            ci.at[p, halo_rows],
-            rh_ss.at[p, d],
-            rh_rs.at[p, lax.rem(turn, HALO)],
+    def swap_copy():
+        return remote(
+            ci.at[own_rows], ci.at[own_rows], sw_ss.at[0], sw_rs.at[0], sibling
+        )
+
+    def row_halo_copy(d):
+        return remote(
+            ci.at[chunk_rows],
+            ci.at[halo_rows],
+            rh_ss.at[d],
+            rh_rs.at[lax.rem(turn, HALO)],
             {"space": lax.rem(z + d, NZ) * 2, "tm": before},
         )
 
-    def row_halo_arrival(p, k):
+    def row_halo_arrival(k):
         at = pl.ds(STEPS + k * CHUNK, CHUNK)
-        return pltpu.make_async_copy(ci.at[p, at], ci.at[p, at], rh_rs.at[p, k])
-
-    def forward_copy(p):
+        return pltpu.make_async_copy(ci.at[at], ci.at[at], rh_rs.at[k])
+
+    def forward_copy():
         at = pl.ds(STEPS, DELAYS)
         return remote(
-            ci.at[p, at], ci.at[p, at], fw_ss.at[p], fw_rs.at[p], sibling
+            ci.at[at], ci.at[at], fw_ss.at[0], fw_rs.at[0], sibling
         )
 
     def scatter_copy(p):
         return remote(
-            ci.at[p, chunk_rows],
+            ci.at[chunk_rows, wide_of(p)],
             cj.at[p, chunk_rows],
             sc_ss.at[p],
             sc_rs.at[p],
@@ -287,7 +290,7 @@
 
     def halo_scatter_copy(p):
         return remote(
-            ci.at[p, chunk_rows], cj.at[p, halo_rows], hs_ss.at[p], hs_rs.at[p], halo_to
+            ci.at[chunk_rows, wide_of(p)], cj.at[p, halo_rows], hs_ss.at[p], hs_rs.at[p], halo_to
         )
 
     def ag_copy(p, d):
@@ -322,21 +325,24 @@
             rs_copy(p, d).wait_recv()
             in_buf = narrow_in if d in NARROW else wide_in
             total = total + in_buf[p, d - 1].astype(jnp.float32)
-        ci[p, chunk_rows] = total.astype(jnp.bfloat16)
+        ci[chunk_rows, wide_of(p)] = total.astype(jnp.bfloat16)
         scatter_copy(p).start()
 
         @pl.when(halo_owner)
         def _():
             halo_scatter_copy(p).start()
 
-    def start_z(p):
+    def start_z():
         for d in ORDER:
-            za_copy(p, d).start()
+            za_copy(d).start()
+
+            @pl.when(halo_owner)
+            def _():
+                row_halo_copy(d).start()
 
         @pl.when(halo_owner)
         def _():
-            for d in ORDER + (0,):
-                row_halo_copy(p, d).start()
+            row_halo_copy(0).start()
 
     def start_plane(p):
         scatter_copy(p).wait_recv()
@@ -350,24 +356,18 @@
             for d in range(NT - 1):
                 ag_halo_copy(p, d).start()
 
-    def finish_z(p):
+    def finish_z():
         for d in ORDER[::-1]:
-            za_copy(p, d).wait_recv()
-        swap_copy(p).start()
+            za_copy(d).wait_recv()
+        swap_copy().start()
 
         @pl.when(jnp.logical_and(core == 0, takes_row_halo))
         def _():
             for k in range(HALO):
-                row_halo_arrival(p, k).wait()
-            forward_copy(p).start()
+                row_halo_arrival(k).wait()
+            forward_copy().start()
 
     def gram(p):
-        swap_copy(p).wait_recv()
-
-        @pl.when(jnp.logical_and(core == 1, takes_row_halo))
-        def _():
-            forward_copy(p).wait_recv()
-
         for d in range(NT - 1)[::-1]:
             ag_copy(p, d).wait_recv()
         for k in range(HALO):
@@ -385,7 +385,7 @@
                 ).wait()
 
         return lax.dot_general(
-            ci[p],
+            ci[:, p * WIDTH : (p + 1) * WIDTH],
             cj[p],
             (((1,), (1,)), ((), ())),
             preferred_element_type=jnp.float32,
@@ -421,44 +421,45 @@
     start_sum(1)
     for p in range(PIECES):
         finish_sum(p)
-    for p in range(PIECES):
-        start_z(p)
+    start_z()
     for p in range(PIECES):
         start_plane(p)
         start_halo(p)
-    for p in range(PIECES):
-        finish_z(p)
+    finish_z()
 
     for p in range(PIECES):
         sib_copy(p).wait_send()
         for d in range(1, NZ):
             rs_copy(p, d).wait_send()
-            za_copy(p, d).wait_send()
         scatter_copy(p).wait_send()
 
         @pl.when(halo_owner)
         def _():
             halo_scatter_copy(p).wait_send()
-            for d in range(NZ):
-                row_halo_copy(p, d).wait_send()
+
+    swap_copy().wait_recv()
+
+    @pl.when(jnp.logical_and(core == 1, takes_row_halo))
+    def _():
+        forward_copy().wait_recv()
 
     window = gram(0)
-    for p in range(1, PIECES):
-        window = window + gram(p)
-    shift = 1
-    while shift < DELAYS:
-        moved = pltpu.roll(window, ROWS - shift, 0)
-        window = window + pltpu.roll(moved, COLS - shift, 1)
-        shift *= 2
-    out[...] = window[:STEPS, :STEPS] * SCALE
+
+    for d in range(1, NZ):
+        za_copy(d).wait_send()
+
+    @pl.when(halo_owner)
+    def _():
+        for d in range(NZ):
+            row_halo_copy(d).wait_send()
+
+    swap_copy().wait_send()
+
+    @pl.when(jnp.logical_and(core == 0, takes_row_halo))
+    def _():
+        forward_copy().wait_send()
 
     for p in range(PIECES):
-        swap_copy(p).wait_send()
-
-        @pl.when(jnp.logical_and(core == 0, takes_row_halo))
-        def _():
-            forward_copy(p).wait_send()
-
         for d in range(NT - 1):
             ag_copy(p, d).wait_send()
 
@@ -467,24 +468,39 @@
             for d in range(NT - 1):
                 ag_halo_copy(p, d).wait_send()
 
+    for p in range(1, PIECES):
+        window = window + gram(p)
+    shift = DELAYS // 2
+    while shift >= 8:
+        rows = window.shape[0] - shift
+        moved = pltpu.roll(window[shift:], COLS - shift, 1)
+        window = window[:rows] + moved
+        shift //= 2
+    while shift >= 1:
+        moved = pltpu.roll(window, window.shape[0] - shift, 0)
+        window = window + pltpu.roll(moved, COLS - shift, 1)
+        shift //= 2
+    out[...] = window[:STEPS, :STEPS] * SCALE
+
 
 def per_device(snapshots, pod_basis):
     dma = pltpu.SemaphoreType.DMA
     f32, bf16 = jnp.float32, jnp.bfloat16
     sems = [dma((KCUT,)), dma((PIECES, KCUT))]
+    two = (PIECES,)
     for sent, received in (
-        ((), ()),
+        (two, two),
+        (two + (NZ - 1,), two + (NZ - 1,)),
         ((NZ - 1,), (NZ - 1,)),
-        ((NZ - 1,), (NZ - 1,)),
-        ((), ()),
+        ((1,), (1,)),
         ((NZ,), (HALO,)),
-        ((), ()),
-        ((), ()),
-        ((), ()),
-        ((NT - 1,), (NT - 1,)),
-        ((NT - 1,), (4,)),
+        ((1,), (1,)),
+        (two, two),
+        (two, two),
+        (two + (NT - 1,), two + (NT - 1,)),
+        (two + (NT - 1,), two + (HALO,)),
     ):
-        sems += [dma((PIECES,) + sent), dma((PIECES,) + received)]
+        sems += [dma(sent), dma(received)]
     return pl.pallas_call(
         kernel,
         out_shape=jax.ShapeDtypeStruct((STEPS, STEPS), f32),
@@ -499,7 +515,7 @@
             pltpu.VMEM((PIECES, NZ - 1, CHUNK, WIDTH), f32),
             pltpu.VMEM((PIECES, OWN, WIDTH), bf16),
             pltpu.VMEM((PIECES, NZ - 1, CHUNK, WIDTH), bf16),
-            pltpu.VMEM((PIECES, ROWS, WIDTH), bf16),
+            pltpu.VMEM((ROWS, MODES), bf16),
             pltpu.VMEM((PIECES, COLS, WIDTH), bf16),
         ]
         + sems,

time: 31.6 us -> 31.1 us (0.984)
  Pallas kernels: 30.9 us -> 30.3 us
    pallas_call x1, Pallas kernels: 30.9 us -> 30.3 us  [per_device(): pl.pallas_call(kernel, out_shape=jax.ShapeDtypeStruct((STEPS, STEPS), f32...]
where the time goes in v4:
time: 31.1 us; the launch traced here: 31 us
  Pallas kernels  30.3 us (97%)
  local copies, waits for them, and re-layouts  0.71 us (2%)
    pallas_call x1, Pallas kernels, per_device(): pl.pallas_call(kernel, out_shape=jax.ShapeDtypeStruct((STEPS, STEPS), f32...  30.3 us
    unnamed x1, local copies, waits for them, and re-layouts  0.71 us

profile of v4, /device:TPU:1, one launch (start us, length us, event | category | flops | bytes accessed | tf_op | source)
XLA Modules:
  0.0 31.0 jit_solution(4593417229826074820)
XLA Ops:
  0.0 30.3 %shard_map.28 = f32[256,256]{1,0:T(8,128)S(1)} custom-call(bf16[8192,256]{1,0:T(8,128)(2,1)} %snap.1, bf16[8192,512]{1,0:T(8,128)(2,1)} %pod.1), custom_call_target="tpu_custom_call" | custom-call | tf_op jit(solution)/shard_map/pallas_call | solution.py:504
  30.3 0.7 %copy.4 = f32[256,256]{1,0:T(8,128)} copy(f32[256,256]{1,0:T(8,128)S(1)} %shard_map.28) | data formatting | bytes 524288

commit v5 on v4

--- a/solution.py
+++ b/solution.py
@@ -18,6 +18,7 @@
 OWN = STEPS // 2
 KCUT = 4
 KC = POINTS // KCUT
+LOAD_AFTER = 0
 SEND_AFTER = 1
 ROWS = STEPS + DELAYS
 COLS = 384
@@ -112,9 +113,6 @@
     for k in range(KCUT):
         snap_copy(k).start()
         pod_copy(0, k).start()
-    for p in range(1, PIECES):
-        for k in range(KCUT):
-            pod_copy(p, k).start()
 
     space = lax.axis_index("space")
     tm = lax.axis_index("tm")
@@ -411,6 +409,9 @@
 
     for k in range(KCUT):
         multiply(0, k)
+        if k == LOAD_AFTER:
+            for later in range(KCUT):
+                pod_copy(1, later).start()
     pl.semaphore_wait(barrier, expected)
     sib_copy(0).start()
     for k in range(KCUT):

time: 31.1 us -> 30.9 us (level)
  no operation moved by 1% of the time
where the time goes in v5:
time: 30.9 us
  Pallas kernels  30.1 us (97%)
  local copies, waits for them, and re-layouts  0.71 us (2%)
    pallas_call x1, Pallas kernels, per_device(): pl.pallas_call(kernel, out_shape=jax.ShapeDtypeStruct((STEPS, STEPS), f32...  30.1 us
    unnamed x1, local copies, waits for them, and re-layouts  0.71 us

profile of v5, /device:TPU:1, one launch (start us, length us, event | category | flops | bytes accessed | tf_op | source)
XLA Modules:
  0.0 30.9 jit_solution(15968530727829516317)
XLA Ops:
  0.0 30.1 %shard_map.28 = f32[256,256]{1,0:T(8,128)S(1)} custom-call(bf16[8192,256]{1,0:T(8,128)(2,1)} %snap.1, bf16[8192,512]{1,0:T(8,128)(2,1)} %pod.1), custom_call_target="tpu_custom_call" | custom-call | tf_op jit(solution)/shard_map/pallas_call | solution.py:505
  30.1 0.7 %copy.4 = f32[256,256]{1,0:T(8,128)} copy(f32[256,256]{1,0:T(8,128)S(1)} %shard_map.28) | data formatting | bytes 524288

commit v6 on v5

--- a/solution.py
+++ b/solution.py
@@ -253,10 +253,10 @@
             z_peer(d),
         )
 
-    def swap_copy():
-        return remote(
-            ci.at[own_rows], ci.at[own_rows], sw_ss.at[0], sw_rs.at[0], sibling
-        )
+    def swap_copy(d):
+        at = turn_of(lax.rem(z + NZ - d, NZ))
+        rows = rows_of((core * NZ + at) * CHUNK, CHUNK)
+        return remote(ci.at[rows], ci.at[rows], sw_ss.at[d], sw_rs.at[d], sibling)
 
     def row_halo_copy(d):
         return remote(
@@ -355,9 +355,10 @@
                 ag_halo_copy(p, d).start()
 
     def finish_z():
+        swap_copy(0).start()
         for d in ORDER[::-1]:
             za_copy(d).wait_recv()
-        swap_copy().start()
+            swap_copy(d).start()
 
         @pl.when(jnp.logical_and(core == 0, takes_row_halo))
         def _():
@@ -438,7 +439,8 @@
         def _():
             halo_scatter_copy(p).wait_send()
 
-    swap_copy().wait_recv()
+    for d in range(NZ):
+        swap_copy(d).wait_recv()
 
     @pl.when(jnp.logical_and(core == 1, takes_row_halo))
     def _():
@@ -454,7 +456,8 @@
         for d in range(NZ):
             row_halo_copy(d).wait_send()
 
-    swap_copy().wait_send()
+    for d in range(NZ):
+        swap_copy(d).wait_send()
 
     @pl.when(jnp.logical_and(core == 0, takes_row_halo))
     def _():
@@ -493,7 +496,7 @@
         (two, two),
         (two + (NZ - 1,), two + (NZ - 1,)),
         ((NZ - 1,), (NZ - 1,)),
-        ((1,), (1,)),
+        ((NZ,), (NZ,)),
         ((NZ,), (HALO,)),
         ((1,), (1,)),
         (two, two),

time: 30.9 us -> 31.1 us (level)
  no operation moved by 1% of the time
where the time goes in v6:
time: 31.1 us; the launch traced here: 31 us
  Pallas kernels  30.3 us (97%)
  local copies, waits for them, and re-layouts  0.71 us (2%)
    pallas_call x1, Pallas kernels, per_device(): pl.pallas_call(kernel, out_shape=jax.ShapeDtypeStruct((STEPS, STEPS), f32...  30.3 us
    unnamed x1, local copies, waits for them, and re-layouts  0.71 us

profile of v6, /device:TPU:1, one launch (start us, length us, event | category | flops | bytes accessed | tf_op | source)
XLA Modules:
  0.0 31.0 jit_solution(3140415111567806541)
XLA Ops:
  0.0 30.3 %shard_map.28 = f32[256,256]{1,0:T(8,128)S(1)} custom-call(bf16[8192,256]{1,0:T(8,128)(2,1)} %snap.1, bf16[8192,512]{1,0:T(8,128)(2,1)} %pod.1), custom_call_target="tpu_custom_call" | custom-call | tf_op jit(solution)/shard_map/pallas_call | solution.py:508
  30.3 0.7 %copy.4 = f32[256,256]{1,0:T(8,128)} copy(f32[256,256]{1,0:T(8,128)S(1)} %shard_map.28) | data formatting | bytes 524288
